TPU v7x, 32 devices: a whole 2x2x4 slice. The times are simulated.
32 devices in a mesh: row: 8 (over z, core), col: 4 (over y, x).
Axes of the slice: x: 2, y: 2, z: 4, core: 2. Of those that a mesh axis runs over, the one named last changes fastest.
Arguments:
- hidden_pre: bfloat16 [512, 16384], P('col', 'row'), may hold values from -6 to 6
- weight_blocks: bfloat16 [8, 4, 8, 256, 256], P('row', 'col'), may hold values from -0.09375 to 0.09375
- block_rows: int32 [8, 4, 8], P('row', 'col'), may hold values from 0 to 63, as said below
- block_cols: int32 [8, 4, 8], P('row', 'col'), may hold values from 0 to 31, as said below
- block_counts: int32 [8, 4], P('row', 'col'), may hold values from 2 to 8, as said below
- out_grad: bfloat16 [512, 8192], P('row', 'col'), may hold values from -6 to 6
Outputs:
- projected: bfloat16 [512, 8192], P('row', 'col')
- grad_hidden: bfloat16 [512, 16384], P('col', 'row')
- grad_blocks: float32 [8, 4, 8, 256, 256], P('row', 'col')
Inputs may be any that keep to these rules, and one draw needn't show every extreme that they name: `block_rows`: owner (r, c) holds only blocks of block-rows r * 8 to (r + 1) * 8 - 1 and block-columns c * 8 to (c + 1) * 8 - 1; the 8 slots of one owner name 8 different blocks. `block_cols`: same owner ranges as block_rows. `block_counts`: some owner holds exactly 8 live blocks and some owner exactly 2.
All inputs are finite; a program needn't handle non-finite values.
Results may differ from a plain program's by a relative error of at most 0.0051.
Values may be sent and summed in bfloat16 or wider, within the bound.
A program may use at most 128 MiB of HBM per device.

v0:
```python
import jax
import jax.numpy as jnp
from jax import lax
from jax.sharding import PartitionSpec as P


def silu_rounded(values):
    return jax.nn.silu(values.astype(jnp.float32)).astype(jnp.bfloat16)


def on_device(hidden_pre, weight_blocks, block_rows, block_cols, block_counts, out_grad):
    width = weight_blocks.shape[-1]
    slot_count = weight_blocks.shape[2]
    row_span = hidden_pre.shape[1] // width
    col_span = out_grad.shape[1] // width
    row_base = lax.axis_index("row") * row_span
    row_local = block_rows[0, 0] - row_base
    col_local = block_cols[0, 0] - lax.axis_index("col") * col_span
    alive = jnp.arange(slot_count, dtype=jnp.int32) < block_counts[0, 0]
    w_live = jnp.where(
        alive[:, None, None], weight_blocks[0, 0], jnp.zeros_like(weight_blocks[0, 0])
    )
    row_pick = (row_local[:, None] == jnp.arange(row_span, dtype=jnp.int32)[None, :]).astype(
        jnp.float32
    )
    col_pick = (col_local[:, None] == jnp.arange(col_span, dtype=jnp.int32)[None, :]).astype(
        jnp.float32
    )
    grad_full = lax.all_gather(out_grad, "row", axis=0, tiled=True)
    act_rows = silu_rounded(lax.all_gather(hidden_pre, "col", axis=0, tiled=True))
    count = act_rows.shape[0]
    a_stack = jnp.take(act_rows.reshape(count, row_span, width), row_local, axis=1)
    prod = jnp.einsum("nkp,kpq->nkq", a_stack, w_live, preferred_element_type=jnp.float32)
    placed = jnp.einsum("nkq,kc->ncq", prod, col_pick, precision=lax.Precision.HIGHEST)
    partial_value = placed.reshape(count, col_span * width)
    grad_rows = grad_full
    act_rows = silu_rounded(lax.all_gather(hidden_pre, "col", axis=0, tiled=True))
    count = act_rows.shape[0]
    a_stack = jnp.take(act_rows.reshape(count, row_span, width), row_local, axis=1)
    g_stack = jnp.take(grad_rows.reshape(count, col_span, width), col_local, axis=1)
    weight_grad = jnp.einsum("nkp,nkq->kpq", a_stack, g_stack, preferred_element_type=jnp.float32)
    projected = lax.psum_scatter(partial_value, "row", scatter_dimension=0, tiled=True).astype(
        jnp.bfloat16
    )
    count = hidden_pre.shape[0] * lax.axis_size("col")
    grad_rows = grad_full
    g_stack = jnp.take(grad_rows.reshape(count, col_span, width), col_local, axis=1)
    back = jnp.einsum("nkq,kpq->nkp", g_stack, w_live, preferred_element_type=jnp.float32)
    placed = jnp.einsum("nkp,kr->nrp", back, row_pick, precision=lax.Precision.HIGHEST)
    back_act = lax.psum_scatter(
        placed.reshape(count, row_span * width), "col", scatter_dimension=0, tiled=True
    )
    hidden_f = hidden_pre.astype(jnp.float32)
    sig = jax.nn.sigmoid(hidden_f)
    grad_hidden = (back_act * (sig * (1.0 + hidden_f * (1.0 - sig)))).astype(jnp.bfloat16)
    grad_blocks = jnp.where(alive[:, None, None], weight_grad, jnp.zeros_like(weight_grad))
    return (projected, grad_hidden, grad_blocks[None, None])


def solution(mesh):
    placed = (
        P("col", "row"),
        P("row", "col", None, None, None),
        P("row", "col", None),
        P("row", "col", None),
        P("row", "col"),
        P("row", "col"),
    )
    return jax.shard_map(
        on_device,
        mesh=mesh,
        in_specs=placed,
        out_specs=(P("row", "col"), P("col", "row"), P("row", "col", None, None, None)),
        check_vma=False,
    )
```

profile of v0, /device:TPU:9, one launch (start us, length us, event | category | flops | bytes accessed | tf_op | source)
XLA Modules:
  0.0 192.0 jit_solution(5066251066862516377)
XLA Ops:
  7.2 2.0 %copy.18 = bf16[128,2048]{0,1:T(8,128)(2,1)} copy(bf16[128,2048]{1,0:T(8,128)(2,1)} %param.8) | data formatting | bytes 1048576 | tf_op args[0]
  9.3 0.7 all-gather.5.cloned.1.call-update
  12.1 34.7 %all-gather.3.cloned.1.call-done = bf16[512,2048]{0,1:T(8,128)(2,1)} async-done(((bf16[128,2048]{0,1:T(8,128)(2,1)}), bf16[512,2048]{0,1:T(8,128)(2,1)}) %all-gather.3.cloned.1.call-update) | async-done | bytes 2097168 | tf_op jit(solution)/shard_map/all_gather | solution.py:30
  46.8 4.1 %fusion.3 = bf16[512,2048]{0,1:T(8,128)(2,1)} fusion(bf16[512,2048]{0,1:T(8,128)(2,1)} %all-gather.3.cloned.1.call-done), kind=kLoop, calls=%fused_computation.7 | loop fusion | flops 6291456 | bytes 4194304 | tf_op jit(solution)/shard_map/convert_element_type | solution.py:8
  50.8 2.8 %copy.19 = bf16[512,8,256]{2,0,1:T(8,128)(2,1)S(1)} copy(bf16[512,8,256]{0,2,1:T(8,128)(2,1)} %bitcast.52) | data formatting | bytes 4194304 | tf_op jit(solution)/shard_map/reshape | solution.py:32
  53.7 2.0 %gather_fusion = bf16[8,512,256]{2,1,0:T(8,128)(2,1)} fusion(bf16[512,8,256]{2,0,1:T(8,128)(2,1)S(1)} %copy.19, s32[1024]{0:T(1024)S(1)} %pad_clamp_fusion.1), kind=kCustom, calls=%fused_computation.clone | custom fusion | bytes 4194336 | tf_op jit(solution)/shard_map/jit(_take)/gather | solution.py:32
  55.7 4.5 %convolution_bitcast_fusion.1 = f32[512,8,256]{0,2,1:T(8,128)} fusion(bf16[8,512,256]{2,1,0:T(8,128)(2,1)} %gather_fusion, pred[8]{0:T(512)(128)(4,1)S(1)} %get-tuple-element.6, bf16[1,1,8,256,256]{4,3,2,1,0:T(8,128)(2,1)S(1)} %copy-done.1, pred[8]{0:T(512)(128)(4,1)S(1)} %get-tuple-element.8), kind=kOutput, calls=%fused_computation.9 | convolution fusion | flops 538443776 | bytes 7340048 | tf_op jit(solution)/shard_map/nkp,kpq->nkq/dot_general | solution.py:33
  60.2 5.5 %copy.21 = f32[512,8,256]{2,1,0:T(8,128)} copy(f32[512,8,256]{0,2,1:T(8,128)} %convolution_bitcast_fusion.1) | data formatting | bytes 8388608 | tf_op jit(solution)/shard_map/nkp,kpq->nkq/transpose | solution.py:33
  65.7 4.3 %fusion.21 = f32[8,512,256]{2,0,1:T(8,128)S(1)} fusion(f32[512,8,256]{2,1,0:T(8,128)} %copy.21, s32[8]{0:T(128)S(1)} %get-tuple-element.5), kind=kOutput, calls=%fused_computation.33 | convolution fusion | flops 100663360 | bytes 8388640 | tf_op jit(solution)/shard_map/nkq,kc->ncq/dot_general | solution.py:34
  70.0 3.9 %copy.28 = f32[64,8,8,256]{3,1,2,0:T(8,128)} copy(f32[64,8,8,256]{3,2,1,0:T(8,128)S(1)} %bitcast.51) | data formatting | bytes 8388608
  74.2 3.7 %all-gather.5.cloned.1.call-done = bf16[512,2048]{1,0:T(8,128)(2,1)} async-done(((bf16[64,2048]{1,0:T(8,128)(2,1)}), bf16[512,2048]{1,0:T(8,128)(2,1)}) %all-gather.5.cloned.1.call-update) | async-done | bytes 2097168 | tf_op jit(solution)/shard_map/all_gather | solution.py:29
  77.9 3.9 %copy.22 = bf16[512,2048]{0,1:T(8,128)(2,1)} copy(bf16[512,2048]{1,0:T(8,128)(2,1)} %all-gather.5.cloned.1.call-done) | data formatting | bytes 4194304 | tf_op jit(solution)/shard_map/all_gather | solution.py:29
  81.8 2.8 %copy.23 = bf16[512,8,256]{2,0,1:T(8,128)(2,1)S(1)} copy(bf16[512,8,256]{0,2,1:T(8,128)(2,1)} %bitcast.53) | data formatting | bytes 4194304 | tf_op jit(solution)/shard_map/reshape | solution.py:47
  84.7 2.0 %gather_fusion.1 = bf16[8,512,256]{2,1,0:T(8,128)(2,1)} fusion(bf16[512,8,256]{2,0,1:T(8,128)(2,1)S(1)} %copy.23, s32[1024]{0:T(1024)S(1)} %pad_clamp_fusion), kind=kCustom, calls=%fused_computation.1.clone | custom fusion | bytes 4194336 | tf_op jit(solution)/shard_map/jit(_take)/gather | solution.py:47
  86.7 4.4 %convolution_bitcast_fusion = f32[512,8,256]{0,2,1:T(8,128)} fusion(bf16[8,512,256]{2,1,0:T(8,128)(2,1)} %gather_fusion.1, pred[8]{0:T(512)(128)(4,1)S(1)} %get-tuple-element.4, bf16[1,1,8,256,256]{4,3,2,1,0:T(8,128)(2,1)S(1)} %copy-done.1, pred[8]{0:T(512)(128)(4,1)S(1)} %get-tuple-element.8), kind=kOutput, calls=%fused_computation.8 | convolution fusion | flops 538443776 | bytes 7340048 | tf_op jit(solution)/shard_map/nkq,kpq->nkp/dot_general | solution.py:48
  91.1 5.5 %copy.24 = f32[512,8,256]{2,1,0:T(8,128)} copy(f32[512,8,256]{0,2,1:T(8,128)} %convolution_bitcast_fusion) | data formatting | bytes 8388608 | tf_op jit(solution)/shard_map/nkq,kpq->nkp/transpose | solution.py:48
  96.5 4.3 %fusion.24 = f32[8,512,256]{2,0,1:T(8,128)S(1)} fusion(f32[512,8,256]{2,1,0:T(8,128)} %copy.24, s32[8]{0:T(128)S(1)} %get-tuple-element.7), kind=kOutput, calls=%fused_computation.35 | convolution fusion | flops 100663360 | bytes 8388640 | tf_op jit(solution)/shard_map/nkp,kr->nrp/dot_general | solution.py:49
  100.8 3.9 %copy.29 = f32[64,8,8,256]{3,1,2,0:T(8,128)} copy(f32[64,8,8,256]{3,2,1,0:T(8,128)S(1)} %bitcast.50) | data formatting | bytes 8388608
  104.8 1.6 copy-done
  106.4 4.0 %select_bitcast_fusion = f32[1,1,8,256,256]{4,3,2,1,0:T(8,128)} fusion(pred[8]{0:T(512)(128)(4,1)S(1)} %get-tuple-element.8, bf16[8,512,256]{2,1,0:T(8,128)(2,1)S(1)} %copy-done, pred[8]{0:T(512)(128)(4,1)S(1)} %get-tuple-element.6, bf16[8,512,256]{2,1,0:T(8,128)(2,1)} %gather_fusion.1, pred[8]{0:T(512)(128)(4,1)S(1)} %get-tuple-element.4), kind=kOutput, calls=%fused_computation.15 | convolution fusion | flops 539492352 | bytes 6291480 | tf_op jit(solution)/shard_map/nkp,nkq->kpq/dot_general | solution.py:41
  110.4 17.4 %reduce-scatter.3.cloned.1.call-done = f32[64,2048]{1,0:T(8,128)} async-done(((f32[512,2048]{1,0:T(8,128)}), f32[64,2048]{1,0:T(8,128)}) %reduce-scatter.3.cloned.1.call-update) | async-done | bytes 524304 | tf_op jit(solution)/shard_map/reduce_scatter | solution.py:42
  127.8 1.8 convert_element_type.21
  129.6 53.5 %reduce-scatter.5.cloned.1.call-done = f32[128,2048]{1,0:T(8,128)} async-done(((f32[512,2048]{1,0:T(8,128)}), f32[128,2048]{1,0:T(8,128)}) %reduce-scatter.5.cloned.1.call-update) | async-done | bytes 1048592 | tf_op jit(solution)/shard_map/reduce_scatter | solution.py:50
  183.0 2.4 %fusion.19 = bf16[128,2048]{1,0:T(8,128)(2,1)} fusion(f32[128,2048]{1,0:T(8,128)} %reduce-scatter.5.cloned.1.call-done, bf16[128,2048]{1,0:T(8,128)(2,1)S(1)} %copy-done.2), kind=kLoop, calls=%fused_computation.26 | loop fusion | flops 2621440 | bytes 2097152 | tf_op jit(solution)/shard_map/convert_element_type | solution.py:55
  (18 shorter events, 1.8 us)
Async XLA Ops:
  7.2 39.6 %all-gather.3.cloned.1.call-start = ((), (), s32[]{:S(2)}) async-start(), calls=%async_computation.2 | async-start | bytes 2621440 | tf_op jit(solution)/shard_map/all_gather | solution.py:30
  9.3 68.6 %all-gather.5.cloned.1.call-start = ((), (), s32[]{:S(2)}) async-start(), calls=%async_computation.4 | async-start | bytes 2359296 | tf_op jit(solution)/shard_map/all_gather | solution.py:29
  10.0 117.8 %reduce-scatter.3.cloned.1.call-start = ((), (), s32[]{:S(2)}) async-start(), calls=%async_computation.3 | async-start | bytes 4718592 | tf_op jit(solution)/shard_map/reduce_scatter | solution.py:42
  53.7 2.0 %copy-start.1 = (bf16[1,1,8,256,256]{4,3,2,1,0:T(8,128)(2,1)S(1)}, bf16[1,1,8,256,256]{4,3,2,1,0:T(8,128)(2,1)}, u32[]{:S(2)}) copy-start(bf16[1,1,8,256,256]{4,3,2,1,0:T(8,128)(2,1)} %param.9) | copy-start | bytes 3145732
  73.9 109.1 %reduce-scatter.5.cloned.1.call-start = ((), (), s32[]{:S(2)}) async-start(), calls=%async_computation.5 | async-start | bytes 5242880 | tf_op jit(solution)/shard_map/reduce_scatter | solution.py:50
  104.7 1.6 copy-start
  106.4 76.7 %copy-start.2 = (bf16[128,2048]{1,0:T(8,128)(2,1)S(1)}, bf16[128,2048]{1,0:T(8,128)(2,1)}, u32[]{:S(2)}) copy-start(bf16[128,2048]{1,0:T(8,128)(2,1)} %param.8) | copy-start | bytes 1572868
Sparse Core Ops, SparseCore 0:
  10.4 36.3 all-gather.2
  48.4 29.4 all-gather.4
  80.2 47.5 reduce-scatter.2
  130.6 52.3 reduce-scatter.4
where the time goes:
time: 194 us; the launch traced here: 192 us
  waiting for transfers between devices  110 us (57%)
  local copies, waits for them, and re-layouts  36.1 us (19%)
  matrix products  21.4 us (11%)
  between operations  14.5 us (7%)
  other arithmetic  9.6 us (5%)
    reduce_scatter x1, waiting for transfers between devices, on_device(): lax.psum_scatter(placed.reshape(count, row_span * width), 'col', scatter_...  53.5 us
    all_gather x1, waiting for transfers between devices, on_device(): lax.all_gather(hidden_pre, 'col', axis=0, tiled=True)  34.7 us
    reduce_scatter x1, waiting for transfers between devices, on_device(): lax.psum_scatter(partial_value, 'row', scatter_dimension=0, tiled=True)  17.4 us
    unnamed x9, local copies, waits for them, and re-layouts  11.5 us
    transpose x1, local copies, waits for them, and re-layouts, on_device(): jnp.einsum('nkp,kpq->nkq', a_stack, w_live, preferred_element_type=jnp.fl...  5.52 us
    transpose x1, local copies, waits for them, and re-layouts, on_device(): jnp.einsum('nkq,kpq->nkp', g_stack, w_live, preferred_element_type=jnp.fl...  5.49 us
    dot_general x1, matrix products, on_device(): jnp.einsum('nkp,kpq->nkq', a_stack, w_live, preferred_element_type=jnp.fl...  4.5 us
    dot_general x1, matrix products, on_device(): jnp.einsum('nkq,kpq->nkp', g_stack, w_live, preferred_element_type=jnp.fl...  4.39 us
  transfers between devices with their start and end apart: 4, of which 4 were waited for; matrix products, arithmetic and copies ran while one was open for 32% of the time, Pallas kernels for 0%

commit v1 on v0

--- a/solution.py
+++ b/solution.py
@@ -1,14 +1,22 @@
+import functools
+
 import jax
 import jax.numpy as jnp
 from jax import lax
+from jax.experimental import pallas as pl
+from jax.experimental.pallas import tpu as pltpu
 from jax.sharding import PartitionSpec as P
+
+MESH = pl.DeviceIdType.MESH
+F32 = jnp.float32
+BF16 = jnp.bfloat16
 
 
 def silu_rounded(values):
     return jax.nn.silu(values.astype(jnp.float32)).astype(jnp.bfloat16)
 
 
-def on_device(hidden_pre, weight_blocks, block_rows, block_cols, block_counts, out_grad):
+def plain_on_device(hidden_pre, weight_blocks, block_rows, block_cols, block_counts, out_grad):
     width = weight_blocks.shape[-1]
     slot_count = weight_blocks.shape[2]
     row_span = hidden_pre.shape[1] // width
@@ -57,6 +65,315 @@
     return (projected, grad_hidden, grad_blocks[None, None])
 
 
+def fused_kernel(
+    hidden_ref, w_ref, rows_ref, cols_ref, count_ref, grad_ref,
+    proj_ref, gh_ref, gb_ref,
+    act_all, g_all, stage, acc, dsilu, bk, rx, ry, r2a, r2b, s2a, s2b,
+    pj, ps, psum, rz, prev_c, last_c, prev_r, last_r,
+    a_send, a_recv, zg_send, zg_recv, zf_send, zf_recv, ps_send, ps_recv,
+    rz_send, rz_recv, b_send, b_recv,
+):
+    slots, width = w_ref.shape[0], w_ref.shape[1]
+    nb = act_all.shape[0]
+    nc = g_all.shape[0]
+    half = nb // 2
+    group = hidden_ref.shape[0]
+    shard = grad_ref.shape[0]
+    row, col = lax.axis_index("row"), lax.axis_index("col")
+    z, core = lax.div(row, 2), lax.rem(row, 2)
+    y, x = lax.div(col, 2), lax.rem(col, 2)
+    x_peer = {"col": y * 2 + 1 - x}
+    y_peer = {"col": (1 - y) * 2 + x}
+    sibling = {"row": z * 2 + 1 - core}
+    group_of = [
+        y * 2 + x,
+        y * 2 + 1 - x,
+        (1 - y) * 2 + x,
+        (1 - y) * 2 + 1 - x,
+    ]
+
+    def chip(offset):
+        return lax.rem(z + offset, 4)
+
+    def z_peer(offset):
+        return {"row": chip(offset) * 2 + core}
+
+    def remote(src, dst, send, recv, to):
+        return pltpu.make_async_remote_copy(
+            src_ref=src, dst_ref=dst, send_sem=send, recv_sem=recv,
+            device_id=to, device_id_type=MESH,
+        )
+
+    barrier = pltpu.get_barrier_semaphore()
+    for peer in (sibling, x_peer, y_peer, z_peer(1), z_peer(2), z_peer(3)):
+        pl.semaphore_signal(barrier, inc=1, device_id=peer, device_id_type=MESH)
+
+    mine = pl.ds(pl.multiple_of(col * group, group), group)
+    own_rows = pl.ds(pl.multiple_of(row * shard, shard), shard)
+    for b in range(nb):
+        v = hidden_ref[:, b * width:(b + 1) * width].astype(F32)
+        act_all[b, mine, :] = (v * (1.0 / (1.0 + jnp.exp(-v)))).astype(BF16)
+    for b in range(nc):
+        g_all[b, own_rows, :] = grad_ref[:, b * width:(b + 1) * width]
+    pl.semaphore_wait(barrier, 6)
+
+    low, high = pl.ds(0, half), pl.ds(half, half)
+
+    def act_view(part, j):
+        return act_all.at[part, pl.ds(pl.multiple_of(j * group, group), group), :]
+
+    def g_view(r):
+        return g_all.at[:, pl.ds(pl.multiple_of(r * shard, shard), shard), :]
+
+    def act_copy(i, part, j, to):
+        return remote(act_view(part, j), act_view(part, j), a_send.at[i], a_recv.at[i], to)
+
+    a_out = [
+        act_copy(0, low, group_of[0], x_peer),
+        act_copy(1, high, group_of[0], y_peer),
+        act_copy(2, high, group_of[0], x_peer),
+        act_copy(3, low, group_of[0], y_peer),
+        act_copy(4, low, group_of[1], y_peer),
+        act_copy(5, high, group_of[2], x_peer),
+    ]
+    a_in = [
+        act_copy(0, low, group_of[1], x_peer),
+        act_copy(1, high, group_of[2], y_peer),
+        act_copy(2, high, group_of[1], x_peer),
+        act_copy(3, low, group_of[2], y_peer),
+        act_copy(4, low, group_of[3], y_peer),
+        act_copy(5, high, group_of[3], x_peer),
+    ]
+    zg_out = [None] + [
+        remote(g_view(row), g_view(row), zg_send.at[o], zg_recv.at[o], z_peer(o))
+        for o in (1, 2, 3)
+    ]
+    zg_in, zf_out, zf_in = [], [], []
+    for o in range(4):
+        got = chip(4 - o) * 2 + core
+        other = chip(4 - o) * 2 + 1 - core
+        zg_in.append(remote(g_view(got), g_view(got), zg_send.at[o], zg_recv.at[o], z_peer(o)))
+        zf_out.append(remote(g_view(got), g_view(got), zf_send.at[o], zf_recv.at[o], sibling))
+        zf_in.append(remote(g_view(other), g_view(other), zf_send.at[o], zf_recv.at[o], sibling))
+
+    for i in range(4):
+        a_out[i].start()
+    zf_out[0].start()
+    for o in (1, 2, 3):
+        zg_out[o].start()
+
+    count = count_ref[0]
+    row_of = [lax.rem(rows_ref[k], nb) for k in range(slots)]
+    col_of = [lax.rem(cols_ref[k], nc) for k in range(slots)]
+    for of, prev, last, span in ((col_of, prev_c, last_c, nc), (row_of, prev_r, last_r, nb)):
+        for k in range(slots):
+            p = jnp.int32(slots)
+            for j in range(k):
+                p = jnp.where(of[j] == of[k], j, p)
+            prev[k] = p
+        for b in range(span):
+            p = jnp.int32(slots)
+            for k in range(slots):
+                p = jnp.where((of[k] == b) & (k < count), k, p)
+            last[b] = p
+    acc[slots] = jnp.zeros(acc.shape[1:], F32)
+
+    def chain(src, slot_of, span, prev, dims):
+        def step(k, carry):
+            a = stage[lax.rem(slot_of[k], span)]
+            prod = lax.dot_general(a, w_ref[k], (dims, ((), ())), preferred_element_type=F32)
+            acc[k] = prod + acc[prev[k]]
+            return carry
+        stage[...] = src
+        lax.fori_loop(0, slots, step, 0, unroll=True)
+
+    def rows_of(j):
+        return pl.ds(pl.multiple_of(j * group, group), group)
+
+    ps_out = []
+
+    def forward(d):
+        chain(act_all[:, rows_of(group_of[d]), :], rows_ref, nb, prev_c, ((1,), (0,)))
+
+        def put(b, carry):
+            pj[d, b] = acc[last_c[b]].astype(BF16)
+            return carry
+        lax.fori_loop(0, nc, put, 0, unroll=True)
+        away = pl.ds(pl.multiple_of((1 - core) * shard, shard), shard)
+        ps_out.append(remote(pj.at[d, :, away, :], ps.at[d], ps_send.at[d], ps_recv.at[d], sibling))
+        ps_out[d].start()
+
+    def rz_copy(d):
+        j = group_of[d]
+        return remote(
+            psum.at[d], rz.at[lax.rem(j - z + 4, 4)], rz_send.at[d],
+            rz_recv.at[lax.rem(j - z + 4, 4)], {"row": j * 2 + core},
+        )
+
+    def finish_forward(d):
+        ps_out[d].wait_recv()
+        keep = pl.ds(pl.multiple_of(core * shard, shard), shard)
+        psum[d] = (pj[d, :, keep, :].astype(F32) + ps[d].astype(F32)).astype(BF16)
+
+        @pl.when(group_of[d] != z)
+        def _():
+            rz_copy(d).start()
+
+    def backward(o):
+        j = chip(4 - o)
+        chain(g_all[:, rows_of(j), :], cols_ref, nc, prev_r, ((1,), (1,)))
+        d = lax.rem(lax.div(j, 2) + y, 2) * 2 + lax.rem(lax.rem(j, 2) + x, 2)
+
+        def put(b, carry):
+            bk[d, b] = acc[last_r[b]].astype(BF16)
+            return carry
+        lax.fori_loop(0, nb, put, 0, unroll=True)
+
+    forward(0)
+    zf_in[0].wait_recv()
+    backward(0)
+    finish_forward(0)
+    a_in[0].wait_recv()
+    a_out[4].start()
+    a_in[1].wait_recv()
+    a_out[5].start()
+    for b in range(nb):
+        v = hidden_ref[:, b * width:(b + 1) * width].astype(F32)
+        s = 1.0 / (1.0 + jnp.exp(-v))
+        dsilu[b] = s * (1.0 + v * (1.0 - s))
+    a_in[2].wait_recv()
+    forward(1)
+    a_in[3].wait_recv()
+    forward(2)
+    finish_forward(1)
+    finish_forward(2)
+    for o in (1, 2, 3):
+        zg_in[o].wait_recv()
+        zf_out[o].start()
+    for o in (1, 2, 3):
+        zf_in[o].wait_recv()
+        backward(o)
+
+    b_out = [
+        remote(bk.at[3, low], rx.at[1], b_send.at[0], b_recv.at[0], x_peer),
+        remote(bk.at[3, high], ry.at[1], b_send.at[1], b_recv.at[1], y_peer),
+        remote(bk.at[1, low], rx.at[0], b_send.at[2], b_recv.at[2], x_peer),
+        remote(bk.at[2, high], ry.at[0], b_send.at[3], b_recv.at[3], y_peer),
+        remote(s2a, r2a, b_send.at[4], b_recv.at[4], y_peer),
+        remote(s2b, r2b, b_send.at[5], b_recv.at[5], x_peer),
+    ]
+    for i in range(4):
+        b_out[i].start()
+    a_in[4].wait_recv()
+    a_in[5].wait_recv()
+    forward(3)
+    finish_forward(3)
+    b_out[0].wait_recv()
+    s2a[...] = (bk[2, low].astype(F32) + rx[1].astype(F32)).astype(BF16)
+    b_out[4].start()
+    b_out[1].wait_recv()
+    s2b[...] = (bk[1, high].astype(F32) + ry[1].astype(F32)).astype(BF16)
+    b_out[5].start()
+
+    def weight_grad(k, carry):
+        a = act_all[lax.rem(rows_ref[k], nb)]
+        g = g_all[lax.rem(cols_ref[k], nc)]
+        value = lax.dot_general(a, g, (((0,), (0,)), ((), ())), preferred_element_type=F32)
+        gb_ref[k] = jnp.where(k < count, value, jnp.zeros_like(value))
+        return carry
+    lax.fori_loop(0, slots, weight_grad, 0, unroll=True)
+
+    for o in (1, 2, 3):
+        remote(rz.at[o], rz.at[o], rz_send.at[o], rz_recv.at[o], z_peer(o)).wait_recv()
+    d = lax.rem(lax.div(z, 2) + y, 2) * 2 + lax.rem(lax.rem(z, 2) + x, 2)
+    for b in range(nc):
+        total = psum[d, b].astype(F32)
+        for o in (1, 2, 3):
+            total = total + rz[o, b].astype(F32)
+        proj_ref[:, b * width:(b + 1) * width] = total.astype(BF16)
+
+    b_out[2].wait_recv()
+    b_out[4].wait_recv()
+    for b in range(half):
+        total = bk[0, b].astype(F32) + rx[0, b].astype(F32) + r2a[b].astype(F32)
+        gh_ref[:, b * width:(b + 1) * width] = (total * dsilu[b]).astype(BF16)
+    b_out[3].wait_recv()
+    b_out[5].wait_recv()
+    for b in range(half):
+        total = bk[0, half + b].astype(F32) + ry[0, b].astype(F32) + r2b[b].astype(F32)
+        gh_ref[:, (half + b) * width:(half + b + 1) * width] = (total * dsilu[half + b]).astype(BF16)
+
+    for copy in a_out + zg_out[1:] + zf_out + ps_out + b_out:
+        copy.wait_send()
+    for d in range(4):
+        @pl.when(group_of[d] != z)
+        def _():
+            rz_copy(d).wait_send()
+
+
+def fused_on_device(hidden_pre, weight_blocks, block_rows, block_cols, block_counts, out_grad):
+    slots, width = weight_blocks.shape[2], weight_blocks.shape[3]
+    group, shard = hidden_pre.shape[0], out_grad.shape[0]
+    nb, nc = hidden_pre.shape[1] // width, out_grad.shape[1] // width
+    tokens = group * lax.axis_size("col")
+    half = nb // 2
+    vmem = pl.BlockSpec(memory_space=pltpu.VMEM)
+    smem = pl.BlockSpec(memory_space=pltpu.SMEM)
+    dma = pltpu.SemaphoreType.DMA
+    out = pl.pallas_call(
+        fused_kernel,
+        out_shape=(
+            jax.ShapeDtypeStruct(out_grad.shape, BF16),
+            jax.ShapeDtypeStruct(hidden_pre.shape, BF16),
+            jax.ShapeDtypeStruct((slots, width, width), F32),
+        ),
+        in_specs=[vmem, vmem, smem, smem, smem, vmem],
+        out_specs=(vmem, vmem, vmem),
+        scratch_shapes=[
+            pltpu.VMEM((nb, tokens, width), BF16),
+            pltpu.VMEM((nc, tokens, width), BF16),
+            pltpu.VMEM((max(nb, nc), group, width), BF16),
+            pltpu.VMEM((slots + 1, group, width), F32),
+            pltpu.VMEM((nb, group, width), F32),
+            pltpu.VMEM((4, nb, group, width), BF16),
+            pltpu.VMEM((2, half, group, width), BF16),
+            pltpu.VMEM((2, half, group, width), BF16),
+            pltpu.VMEM((half, group, width), BF16),
+            pltpu.VMEM((half, group, width), BF16),
+            pltpu.VMEM((half, group, width), BF16),
+            pltpu.VMEM((half, group, width), BF16),
+            pltpu.VMEM((4, nc, group, width), BF16),
+            pltpu.VMEM((4, nc, shard, width), BF16),
+            pltpu.VMEM((4, nc, shard, width), BF16),
+            pltpu.VMEM((4, nc, shard, width), BF16),
+            pltpu.SMEM((slots,), jnp.int32),
+            pltpu.SMEM((nc,), jnp.int32),
+            pltpu.SMEM((slots,), jnp.int32),
+            pltpu.SMEM((nb,), jnp.int32),
+            dma((6,)), dma((6,)), dma((4,)), dma((4,)), dma((4,)), dma((4,)),
+            dma((4,)), dma((4,)), dma((4,)), dma((4,)), dma((6,)), dma((6,)),
+        ],
+        compiler_params=pltpu.CompilerParams(
+            collective_id=0, has_side_effects=True, vmem_limit_bytes=44 * 1024 * 1024
+        ),
+    )(
+        hidden_pre, weight_blocks[0, 0], block_rows[0, 0], block_cols[0, 0],
+        block_counts[0], out_grad,
+    )
+    return out[0], out[1], out[2][None, None]
+
+
+def on_device(hidden_pre, weight_blocks, block_rows, block_cols, block_counts, out_grad):
+    fits = (
+        lax.axis_size("row") == 8
+        and lax.axis_size("col") == 4
+        and hidden_pre.shape[0] == 2 * out_grad.shape[0]
+        and hidden_pre.shape[1] == out_grad.shape[1]
+    )
+    body = fused_on_device if fits else plain_on_device
+    return body(hidden_pre, weight_blocks, block_rows, block_cols, block_counts, out_grad)
+
+
 def solution(mesh):
     placed = (
         P("col", "row"),

time: 194 us -> 70 us (0.36)
  waiting for transfers between devices: 110 us -> 0 us
  Pallas kernels: 0 us -> 60.9 us
  local copies, waits for them, and re-layouts: 36.1 us -> 7.33 us
  matrix products: 21.4 us -> 0 us
  between operations: 14.5 us -> 1.3 us
  other arithmetic: 9.6 us -> 0 us
    reduce_scatter x2 -> x0, waiting for transfers between devices: 70.9 us -> none  [the longest x1 53.5 us: on_device(): lax.psum_scatter(placed.reshape(count, row_span * width), 'col', scatter_...]
    pallas_call x0 -> x1, Pallas kernels: none -> 60.9 us  [fused_on_device(): pl.pallas_call(fused_kernel, out_shape=(jax.ShapeDtypeStruct(out_grad.sha...]
    all_gather x2 -> x0, waiting for transfers between devices: 38.4 us -> none  [the longest x1 34.7 us: on_device(): lax.all_gather(hidden_pre, 'col', axis=0, tiled=True)]
    dot_general x5 -> x0, matrix products: 21.4 us -> none  [the longest x1 4.5 us: on_device(): jnp.einsum('nkp,kpq->nkq', a_stack, w_live, preferred_element_type=jnp.fl...]
    transpose x2 -> x0, local copies, waits for them, and re-layouts: 11 us -> none  [the longest x1 5.52 us: on_device(): jnp.einsum('nkp,kpq->nkq', a_stack, w_live, preferred_element_type=jnp.fl...]
    convert_element_type x3 -> x0, other arithmetic: 8.25 us -> none  [the longest x1 4.07 us: silu_rounded(): return jax.nn.silu(values.astype(jnp.float32)).astype(jnp.bfloat16)]
    reshape x2 -> x0, local copies, waits for them, and re-layouts: 5.69 us -> none  [the longest x1 2.85 us: on_device(): act_rows.reshape(count, row_span, width)]
    unnamed x9 -> x13, local copies, waits for them, and re-layouts: 11.5 us -> 7.33 us
  transfers between devices with their start and end apart: 4 -> 0, of which waited for: 4 -> 0; matrix products, arithmetic and copies ran while one was open for 32% -> 0% of each run, Pallas kernels for 0% -> 0%
where the time goes in v1:
time: 70 us; the launch traced here: 69.6 us
  Pallas kernels  60.9 us (87%)
  local copies, waits for them, and re-layouts  7.33 us (10%)
  between operations  1.3 us (2%)
    pallas_call x1, Pallas kernels, fused_on_device(): pl.pallas_call(fused_kernel, out_shape=(jax.ShapeDtypeStruct(out_grad.sha...  60.9 us
    unnamed x13, local copies, waits for them, and re-layouts  7.33 us

profile of v1, /device:TPU:9, one launch (start us, length us, event | category | flops | bytes accessed | tf_op | source)
XLA Modules:
  0.0 69.6 jit_solution(8917160996636521067)
XLA Ops:
  1.3 0.0 copy-start
  1.3 1.2 %copy-done = bf16[1,1,8,256,256]{4,3,2,1,0:T(8,128)(2,1)S(1)} copy-done((bf16[1,1,8,256,256]{4,3,2,1,0:T(8,128)(2,1)S(1)}, bf16[1,1,8,256,256]{4,3,2,1,0:T(8,128)(2,1)}, u32[]{:S(2)}) %copy-start) | copy-done | bytes 1048600
  2.5 0.0 copy-start.1
  2.5 1.0 %copy-done.1 = bf16[128,2048]{1,0:T(8,128)(2,1)S(1)} copy-done((bf16[128,2048]{1,0:T(8,128)(2,1)S(1)}, bf16[128,2048]{1,0:T(8,128)(2,1)}, u32[]{:S(2)}) %copy-start.1) | copy-done | bytes 524312
  3.5 0.0 copy-start.2
  3.5 0.9 %copy-done.2 = bf16[64,2048]{1,0:T(8,128)(2,1)S(1)} copy-done((bf16[64,2048]{1,0:T(8,128)(2,1)S(1)}, bf16[64,2048]{1,0:T(8,128)(2,1)}, u32[]{:S(2)}) %copy-start.2) | copy-done | bytes 262168
  4.5 0.0 copy-start.3
  4.5 0.7 copy-done.3
  5.2 0.0 copy-start.4
  5.2 0.7 copy-done.4
  5.8 60.9 %shard_map.85 = (bf16[64,2048]{1,0:T(8,128)(2,1)S(1)}, bf16[128,2048]{1,0:T(8,128)(2,1)S(1)}, f32[8,256,256]{2,1,0:T(8,128)S(1)}) custom-call(bf16[128,2048]{1,0:T(8,128)(2,1)S(1)} %copy-done.1, bf16[8,256,256]{2,1,0:T(8,128)(2,1)S(1)} %bitcast.7, s32[8]{0:T(128)S(1)} %bitcast.8, s32[8]{0:T(128)S(1)} %bitcast.9, s32[1]{0:T(128)} %bitcast.5.count_ref, ...), custom_call_target="tpu_custom_call" | custom-call | tf_op jit(solution)/shard_map/pallas_call | solution.py:323
  66.7 0.7 %copy.13 = bf16[64,2048]{1,0:T(8,128)(2,1)} copy(bf16[64,2048]{1,0:T(8,128)(2,1)S(1)} %get-tuple-element.12) | data formatting | bytes 524288
  67.4 0.8 %copy.14 = bf16[128,2048]{1,0:T(8,128)(2,1)} copy(bf16[128,2048]{1,0:T(8,128)(2,1)S(1)} %get-tuple-element.13) | data formatting | bytes 1048576
  68.2 1.3 %copy.15 = f32[1,1,8,256,256]{4,3,2,1,0:T(8,128)} copy(f32[1,1,8,256,256]{4,3,2,1,0:T(8,128)S(1)} %bitcast.6) | data formatting | bytes 4194304
Async XLA Ops:
  1.3 1.2 %copy-start = (bf16[1,1,8,256,256]{4,3,2,1,0:T(8,128)(2,1)S(1)}, bf16[1,1,8,256,256]{4,3,2,1,0:T(8,128)(2,1)}, u32[]{:S(2)}) copy-start(bf16[1,1,8,256,256]{4,3,2,1,0:T(8,128)(2,1)} %param.7) | copy-start | bytes 3145732
  2.5 1.0 %copy-start.1 = (bf16[128,2048]{1,0:T(8,128)(2,1)S(1)}, bf16[128,2048]{1,0:T(8,128)(2,1)}, u32[]{:S(2)}) copy-start(bf16[128,2048]{1,0:T(8,128)(2,1)} %hidden_ref.1) | copy-start | bytes 1572868
  3.5 0.9 %copy-start.2 = (bf16[64,2048]{1,0:T(8,128)(2,1)S(1)}, bf16[64,2048]{1,0:T(8,128)(2,1)}, u32[]{:S(2)}) copy-start(bf16[64,2048]{1,0:T(8,128)(2,1)} %grad_ref.1) | copy-start | bytes 786436
  4.5 0.7 copy-start.3
  5.2 0.7 copy-start.4

commit v2 on v1

--- a/solution.py
+++ b/solution.py
@@ -14,6 +14,16 @@
 
 def silu_rounded(values):
     return jax.nn.silu(values.astype(jnp.float32)).astype(jnp.bfloat16)
+
+
+def pick_blocks(blocks, which):
+    return jnp.stack(
+        [
+            lax.dynamic_index_in_dim(blocks, which[k], axis=1, keepdims=False)
+            for k in range(which.shape[0])
+        ],
+        axis=1,
+    )
 
 
 def plain_on_device(hidden_pre, weight_blocks, block_rows, block_cols, block_counts, out_grad):
@@ -37,22 +47,22 @@
     grad_full = lax.all_gather(out_grad, "row", axis=0, tiled=True)
     act_rows = silu_rounded(lax.all_gather(hidden_pre, "col", axis=0, tiled=True))
     count = act_rows.shape[0]
-    a_stack = jnp.take(act_rows.reshape(count, row_span, width), row_local, axis=1)
+    a_stack = pick_blocks(act_rows.reshape(count, row_span, width), row_local)
     prod = jnp.einsum("nkp,kpq->nkq", a_stack, w_live, preferred_element_type=jnp.float32)
     placed = jnp.einsum("nkq,kc->ncq", prod, col_pick, precision=lax.Precision.HIGHEST)
     partial_value = placed.reshape(count, col_span * width)
     grad_rows = grad_full
     act_rows = silu_rounded(lax.all_gather(hidden_pre, "col", axis=0, tiled=True))
     count = act_rows.shape[0]
-    a_stack = jnp.take(act_rows.reshape(count, row_span, width), row_local, axis=1)
-    g_stack = jnp.take(grad_rows.reshape(count, col_span, width), col_local, axis=1)
+    a_stack = pick_blocks(act_rows.reshape(count, row_span, width), row_local)
+    g_stack = pick_blocks(grad_rows.reshape(count, col_span, width), col_local)
     weight_grad = jnp.einsum("nkp,nkq->kpq", a_stack, g_stack, preferred_element_type=jnp.float32)
     projected = lax.psum_scatter(partial_value, "row", scatter_dimension=0, tiled=True).astype(
         jnp.bfloat16
     )
     count = hidden_pre.shape[0] * lax.axis_size("col")
     grad_rows = grad_full
-    g_stack = jnp.take(grad_rows.reshape(count, col_span, width), col_local, axis=1)
+    g_stack = pick_blocks(grad_rows.reshape(count, col_span, width), col_local)
     back = jnp.einsum("nkq,kpq->nkp", g_stack, w_live, preferred_element_type=jnp.float32)
     placed = jnp.einsum("nkp,kr->nrp", back, row_pick, precision=lax.Precision.HIGHEST)
     back_act = lax.psum_scatter(
@@ -66,17 +76,20 @@
 
 
 def fused_kernel(
-    hidden_ref, w_ref, rows_ref, cols_ref, count_ref, grad_ref,
+    hidden_hbm, w_hbm, rows_hbm, cols_hbm, count_hbm, grad_hbm,
     proj_ref, gh_ref, gb_ref,
+    hidden_ref, w_buf, rows_buf, cols_buf, count_buf, grad_ref, in_sem,
     act_all, g_all, stage, acc, dsilu, bk, rx, ry, r2a, r2b, s2a, s2b,
-    pj, ps, psum, rz, prev_c, last_c, prev_r, last_r,
+    pj, ps, psum, ch, prev_c, last_c, prev_r, last_r,
     a_send, a_recv, zg_send, zg_recv, zf_send, zf_recv, ps_send, ps_recv,
-    rz_send, rz_recv, b_send, b_recv,
+    c_send, c_recv, b_send, b_recv,
 ):
-    slots, width = w_ref.shape[0], w_ref.shape[1]
+    w_ref, rows_ref, cols_ref = w_buf.at[0, 0], rows_buf.at[0, 0], cols_buf.at[0, 0]
+    slots, width = w_buf.shape[2], w_buf.shape[3]
     nb = act_all.shape[0]
     nc = g_all.shape[0]
     half = nb // 2
+    split = half * width
     group = hidden_ref.shape[0]
     shard = grad_ref.shape[0]
     row, col = lax.axis_index("row"), lax.axis_index("col")
@@ -104,18 +117,31 @@
             device_id=to, device_id_type=MESH,
         )
 
+    ins = [
+        pltpu.make_async_copy(src, dst, in_sem.at[i])
+        for i, (src, dst) in enumerate((
+            (hidden_hbm.at[:, pl.ds(0, split)], hidden_ref.at[:, pl.ds(0, split)]),
+            (hidden_hbm.at[:, pl.ds(split, split)], hidden_ref.at[:, pl.ds(split, split)]),
+            (grad_hbm, grad_ref),
+            (rows_hbm, rows_buf),
+            (cols_hbm, cols_buf),
+            (count_hbm, count_buf),
+            (w_hbm, w_buf),
+        ))
+    ]
+    for copy in ins:
+        copy.start()
     barrier = pltpu.get_barrier_semaphore()
     for peer in (sibling, x_peer, y_peer, z_peer(1), z_peer(2), z_peer(3)):
         pl.semaphore_signal(barrier, inc=1, device_id=peer, device_id_type=MESH)
 
     mine = pl.ds(pl.multiple_of(col * group, group), group)
     own_rows = pl.ds(pl.multiple_of(row * shard, shard), shard)
-    for b in range(nb):
-        v = hidden_ref[:, b * width:(b + 1) * width].astype(F32)
-        act_all[b, mine, :] = (v * (1.0 / (1.0 + jnp.exp(-v)))).astype(BF16)
-    for b in range(nc):
-        g_all[b, own_rows, :] = grad_ref[:, b * width:(b + 1) * width]
-    pl.semaphore_wait(barrier, 6)
+
+    def activate(blocks):
+        for b in blocks:
+            v = hidden_ref[:, b * width:(b + 1) * width].astype(F32)
+            act_all[b, mine, :] = (v * (1.0 / (1.0 + jnp.exp(-v)))).astype(BF16)
 
     low, high = pl.ds(0, half), pl.ds(half, half)
 
@@ -156,13 +182,25 @@
         zf_out.append(remote(g_view(got), g_view(got), zf_send.at[o], zf_recv.at[o], sibling))
         zf_in.append(remote(g_view(other), g_view(other), zf_send.at[o], zf_recv.at[o], sibling))
 
-    for i in range(4):
-        a_out[i].start()
+    ins[0].wait()
+    activate(range(half))
+    pl.semaphore_wait(barrier, 6)
+    a_out[0].start()
+    a_out[3].start()
+    ins[2].wait()
+    for b in range(nc):
+        g_all[b, own_rows, :] = grad_ref[:, b * width:(b + 1) * width]
     zf_out[0].start()
     for o in (1, 2, 3):
         zg_out[o].start()
-
-    count = count_ref[0]
+    ins[1].wait()
+    activate(range(half, nb))
+    a_out[1].start()
+    a_out[2].start()
+    for copy in ins[3:]:
+        copy.wait()
+
+    count = count_buf[0, 0]
     row_of = [lax.rem(rows_ref[k], nb) for k in range(slots)]
     col_of = [lax.rem(cols_ref[k], nc) for k in range(slots)]
     for of, prev, last, span in ((col_of, prev_c, last_c, nc), (row_of, prev_r, last_r, nb)):
@@ -203,21 +241,28 @@
         ps_out.append(remote(pj.at[d, :, away, :], ps.at[d], ps_send.at[d], ps_recv.at[d], sibling))
         ps_out[d].start()
 
-    def rz_copy(d):
+    def advance(d, hop):
         j = group_of[d]
-        return remote(
-            psum.at[d], rz.at[lax.rem(j - z + 4, 4)], rz_send.at[d],
-            rz_recv.at[lax.rem(j - z + 4, 4)], {"row": j * 2 + core},
-        )
-
-    def finish_forward(d):
+        way = jnp.where(j > z, 0, 1)
+        place = jnp.where(j > z, z, 3 - z)
+        onward = {"row": (z + 1 - 2 * way) * 2 + core}
+
+        @pl.when((j != z) & (place == hop))
+        def _():
+            keep = pl.ds(pl.multiple_of(core * shard, shard), shard)
+            total = pj[d, :, keep, :].astype(F32) + ps[d].astype(F32)
+            copy = remote(
+                psum.at[d], ch.at[way, d], c_send.at[d], c_recv.at[way, d], onward
+            )
+            if hop > 0:
+                copy.wait_recv()
+                total = total + ch[way, d].astype(F32)
+            psum[d] = total.astype(BF16)
+            copy.start()
+
+    def pair_sum(d):
         ps_out[d].wait_recv()
-        keep = pl.ds(pl.multiple_of(core * shard, shard), shard)
-        psum[d] = (pj[d, :, keep, :].astype(F32) + ps[d].astype(F32)).astype(BF16)
-
-        @pl.when(group_of[d] != z)
-        def _():
-            rz_copy(d).start()
+        advance(d, 0)
 
     def backward(o):
         j = chip(4 - o)
@@ -232,7 +277,7 @@
     forward(0)
     zf_in[0].wait_recv()
     backward(0)
-    finish_forward(0)
+    pair_sum(0)
     a_in[0].wait_recv()
     a_out[4].start()
     a_in[1].wait_recv()
@@ -245,8 +290,9 @@
     forward(1)
     a_in[3].wait_recv()
     forward(2)
-    finish_forward(1)
-    finish_forward(2)
+    pair_sum(1)
+    pair_sum(2)
+    advance(0, 1)
     for o in (1, 2, 3):
         zg_in[o].wait_recv()
         zf_out[o].start()
@@ -267,7 +313,13 @@
     a_in[4].wait_recv()
     a_in[5].wait_recv()
     forward(3)
-    finish_forward(3)
+    advance(0, 2)
+    advance(1, 1)
+    advance(2, 1)
+    pair_sum(3)
+    advance(1, 2)
+    advance(2, 2)
+    advance(3, 1)
     b_out[0].wait_recv()
     s2a[...] = (bk[2, low].astype(F32) + rx[1].astype(F32)).astype(BF16)
     b_out[4].start()
@@ -283,13 +335,25 @@
         return carry
     lax.fori_loop(0, slots, weight_grad, 0, unroll=True)
 
-    for o in (1, 2, 3):
-        remote(rz.at[o], rz.at[o], rz_send.at[o], rz_recv.at[o], z_peer(o)).wait_recv()
+    advance(3, 2)
     d = lax.rem(lax.div(z, 2) + y, 2) * 2 + lax.rem(lax.rem(z, 2) + x, 2)
+
+    def arrived(way, edge):
+        @pl.when(z == edge)
+        def _():
+            ch[way, d] = jnp.zeros(ch.shape[2:], BF16)
+
+        @pl.when(z != edge)
+        def _():
+            remote(
+                ch.at[way, d], ch.at[way, d], c_send.at[d], c_recv.at[way, d], sibling
+            ).wait_recv()
+    arrived(0, 0)
+    arrived(1, 3)
+    keep = pl.ds(pl.multiple_of(core * shard, shard), shard)
     for b in range(nc):
-        total = psum[d, b].astype(F32)
-        for o in (1, 2, 3):
-            total = total + rz[o, b].astype(F32)
+        total = pj[d, b, keep, :].astype(F32) + ps[d, b].astype(F32)
+        total = total + ch[0, d, b].astype(F32) + ch[1, d, b].astype(F32)
         proj_ref[:, b * width:(b + 1) * width] = total.astype(BF16)
 
     b_out[2].wait_recv()
@@ -308,7 +372,9 @@
     for d in range(4):
         @pl.when(group_of[d] != z)
         def _():
-            rz_copy(d).wait_send()
+            remote(
+                psum.at[d], ch.at[0, d], c_send.at[d], c_recv.at[0, d], sibling
+            ).wait_send()
 
 
 def fused_on_device(hidden_pre, weight_blocks, block_rows, block_cols, block_counts, out_grad):
@@ -318,7 +384,6 @@
     tokens = group * lax.axis_size("col")
     half = nb // 2
     vmem = pl.BlockSpec(memory_space=pltpu.VMEM)
-    smem = pl.BlockSpec(memory_space=pltpu.SMEM)
     dma = pltpu.SemaphoreType.DMA
     out = pl.pallas_call(
         fused_kernel,
@@ -327,9 +392,16 @@
             jax.ShapeDtypeStruct(hidden_pre.shape, BF16),
             jax.ShapeDtypeStruct((slots, width, width), F32),
         ),
-        in_specs=[vmem, vmem, smem, smem, smem, vmem],
+        in_specs=[pl.BlockSpec(memory_space=pl.ANY)] * 6,
         out_specs=(vmem, vmem, vmem),
         scratch_shapes=[
+            pltpu.VMEM(hidden_pre.shape, BF16),
+            pltpu.VMEM(weight_blocks.shape, BF16),
+            pltpu.SMEM(block_rows.shape, jnp.int32),
+            pltpu.SMEM(block_cols.shape, jnp.int32),
+            pltpu.SMEM(block_counts.shape, jnp.int32),
+            pltpu.VMEM(out_grad.shape, BF16),
+            dma((7,)),
             pltpu.VMEM((nb, tokens, width), BF16),
             pltpu.VMEM((nc, tokens, width), BF16),
             pltpu.VMEM((max(nb, nc), group, width), BF16),
@@ -345,20 +417,19 @@
             pltpu.VMEM((4, nc, group, width), BF16),
             pltpu.VMEM((4, nc, shard, width), BF16),
             pltpu.VMEM((4, nc, shard, width), BF16),
-            pltpu.VMEM((4, nc, shard, width), BF16),
+            pltpu.VMEM((2, 4, nc, shard, width), BF16),
             pltpu.SMEM((slots,), jnp.int32),
             pltpu.SMEM((nc,), jnp.int32),
             pltpu.SMEM((slots,), jnp.int32),
             pltpu.SMEM((nb,), jnp.int32),
             dma((6,)), dma((6,)), dma((4,)), dma((4,)), dma((4,)), dma((4,)),
-            dma((4,)), dma((4,)), dma((4,)), dma((4,)), dma((6,)), dma((6,)),
+            dma((4,)), dma((4,)), dma((4,)), dma((2, 4)), dma((6,)), dma((6,)),
         ],
         compiler_params=pltpu.CompilerParams(
-            collective_id=0, has_side_effects=True, vmem_limit_bytes=44 * 1024 * 1024
+            collective_id=0, has_side_effects=True, vmem_limit_bytes=56 * 1024 * 1024
         ),
     )(
-        hidden_pre, weight_blocks[0, 0], block_rows[0, 0], block_cols[0, 0],
-        block_counts[0], out_grad,
+        hidden_pre, weight_blocks, block_rows, block_cols, block_counts, out_grad
     )
     return out[0], out[1], out[2][None, None]
 

time: 70 us -> 63.3 us (0.904)
  the two profiles are of different devices: /device:TPU:9 before, /device:TPU:24 now
where the time goes in v2:
time: 63.3 us; the launch traced here: 63 us
  Pallas kernels  55.2 us (87%)
  local copies, waits for them, and re-layouts  6.59 us (10%)
  between operations  1.29 us (2%)
    pallas_call x1, Pallas kernels, fused_on_device(): pl.pallas_call(fused_kernel, out_shape=(jax.ShapeDtypeStruct(out_grad.sha...  55.2 us
    unnamed x3, local copies, waits for them, and re-layouts  6.59 us

profile of v2, /device:TPU:24, one launch (start us, length us, event | category | flops | bytes accessed | tf_op | source)
XLA Modules:
  0.0 63.0 jit_solution(16181414204561691952)
XLA Ops:
  1.3 55.2 %shard_map.85 = (bf16[64,2048]{1,0:T(8,128)(2,1)}, bf16[128,2048]{1,0:T(8,128)(2,1)}, f32[8,256,256]{2,1,0:T(8,128)}) custom-call(bf16[128,2048]{1,0:T(8,128)(2,1)} %hidden_hbm.1, bf16[1,1,8,256,256]{4,3,2,1,0:T(8,128)(2,1)} %w_hbm.1, s32[1,1,8]{2,1,0:T(1,128)} %rows_hbm.1, s32[1,1,8]{2,1,0:T(1,128)} %cols_hbm.1, s32[1,1]{1,0:T(1,128)S(6)} %copy.12.count_hbm, ...), custom_call_target="tpu_custom_call" | custom-call | tf_op jit(solution)/shard_map/pallas_call | solution.py:388
  56.4 1.7 %copy.13 = bf16[64,2048]{1,0:T(8,128)(2,1)} copy(bf16[64,2048]{1,0:T(8,128)(2,1)} %get-tuple-element.12) | data formatting | bytes 524288
  58.1 1.9 %copy.14 = bf16[128,2048]{1,0:T(8,128)(2,1)} copy(bf16[128,2048]{1,0:T(8,128)(2,1)} %get-tuple-element.13) | data formatting | bytes 1048576
  60.0 3.0 %copy.15 = f32[1,1,8,256,256]{4,3,2,1,0:T(8,128)} copy(f32[1,1,8,256,256]{4,3,2,1,0:T(8,128)} %bitcast.1) | data formatting | bytes 4194304

commit v3 on v2

--- a/solution.py
+++ b/solution.py
@@ -90,6 +90,8 @@
     nc = g_all.shape[0]
     half = nb // 2
     split = half * width
+    pieces = 4
+    piece = nc // pieces
     group = hidden_ref.shape[0]
     shard = grad_ref.shape[0]
     row, col = lax.axis_index("row"), lax.axis_index("col")
@@ -250,15 +252,18 @@
         @pl.when((j != z) & (place == hop))
         def _():
             keep = pl.ds(pl.multiple_of(core * shard, shard), shard)
-            total = pj[d, :, keep, :].astype(F32) + ps[d].astype(F32)
-            copy = remote(
-                psum.at[d], ch.at[way, d], c_send.at[d], c_recv.at[way, d], onward
-            )
-            if hop > 0:
-                copy.wait_recv()
-                total = total + ch[way, d].astype(F32)
-            psum[d] = total.astype(BF16)
-            copy.start()
+            for c in range(pieces):
+                part = pl.ds(c * piece, piece)
+                total = pj[d, part, keep, :].astype(F32) + ps[d, part].astype(F32)
+                copy = remote(
+                    psum.at[d, part], ch.at[way, d, part], c_send.at[d, c],
+                    c_recv.at[way, d, c], onward,
+                )
+                if hop > 0:
+                    copy.wait_recv()
+                    total = total + ch[way, d, part].astype(F32)
+                psum[d, part] = total.astype(BF16)
+                copy.start()
 
     def pair_sum(d):
         ps_out[d].wait_recv()
@@ -345,9 +350,9 @@
 
         @pl.when(z != edge)
         def _():
-            remote(
-                ch.at[way, d], ch.at[way, d], c_send.at[d], c_recv.at[way, d], sibling
-            ).wait_recv()
+            for c in range(pieces):
+                got = ch.at[way, d, pl.ds(c * piece, piece)]
+                remote(got, got, c_send.at[d, c], c_recv.at[way, d, c], sibling).wait_recv()
     arrived(0, 0)
     arrived(1, 3)
     keep = pl.ds(pl.multiple_of(core * shard, shard), shard)
@@ -372,9 +377,45 @@
     for d in range(4):
         @pl.when(group_of[d] != z)
         def _():
-            remote(
-                psum.at[d], ch.at[0, d], c_send.at[d], c_recv.at[0, d], sibling
-            ).wait_send()
+            for c in range(pieces):
+                part = pl.ds(c * piece, piece)
+                remote(
+                    psum.at[d, part], ch.at[0, d, part], c_send.at[d, c],
+                    c_recv.at[0, d, c], sibling,
+                ).wait_send()
+
+
+def hand_on_kernel(p_in, h_in, b_in, p_out, h_out, b_out, p_buf, h_buf, b_buf, i_sem, o_sem):
+    pairs = [(p_in, p_buf, p_out), (h_in, h_buf, h_out)]
+    for k in range(b_in.shape[0]):
+        pairs.append((b_in.at[k], b_buf.at[k], b_out.at[k]))
+    fetches = [
+        pltpu.make_async_copy(src, buf, i_sem.at[i]) for i, (src, buf, dst) in enumerate(pairs)
+    ]
+    stores = [
+        pltpu.make_async_copy(buf, dst, o_sem.at[i]) for i, (src, buf, dst) in enumerate(pairs)
+    ]
+    for fetch in fetches:
+        fetch.start()
+    for fetch, store in zip(fetches, stores):
+        fetch.wait()
+        store.start()
+    for store in stores:
+        store.wait()
+
+
+def hand_on(proj, grad_hidden, grad_blocks):
+    whole = pl.BlockSpec(memory_space=pl.ANY)
+    arrays = (proj, grad_hidden, grad_blocks)
+    return pl.pallas_call(
+        hand_on_kernel,
+        out_shape=tuple(jax.ShapeDtypeStruct(a.shape, a.dtype) for a in arrays),
+        in_specs=[whole] * 3,
+        out_specs=(whole,) * 3,
+        scratch_shapes=[pltpu.VMEM(a.shape, a.dtype) for a in arrays]
+        + [pltpu.SemaphoreType.DMA((2 + grad_blocks.shape[0],))] * 2,
+        compiler_params=pltpu.CompilerParams(vmem_limit_bytes=56 * 1024 * 1024),
+    )(*arrays)
 
 
 def fused_on_device(hidden_pre, weight_blocks, block_rows, block_cols, block_counts, out_grad):
@@ -423,7 +464,7 @@
             pltpu.SMEM((slots,), jnp.int32),
             pltpu.SMEM((nb,), jnp.int32),
             dma((6,)), dma((6,)), dma((4,)), dma((4,)), dma((4,)), dma((4,)),
-            dma((4,)), dma((4,)), dma((4,)), dma((2, 4)), dma((6,)), dma((6,)),
+            dma((4,)), dma((4,)), dma((4, 4)), dma((2, 4, 4)), dma((6,)), dma((6,)),
         ],
         compiler_params=pltpu.CompilerParams(
             collective_id=0, has_side_effects=True, vmem_limit_bytes=56 * 1024 * 1024
@@ -431,7 +472,8 @@
     )(
         hidden_pre, weight_blocks, block_rows, block_cols, block_counts, out_grad
     )
-    return out[0], out[1], out[2][None, None]
+    outs = hand_on(*out)
+    return outs[0], outs[1], outs[2][None, None]
 
 
 def on_device(hidden_pre, weight_blocks, block_rows, block_cols, block_counts, out_grad):

time: 63.3 us -> 56.9 us (0.90)
  the two profiles are of different devices: /device:TPU:24 before, /device:TPU:9 now
where the time goes in v3:
time: 56.9 us; the launch traced here: 56.7 us
  Pallas kernels  55.4 us (97%)
  between operations  1.29 us (2%)
    pallas_call x1, Pallas kernels, fused_on_device(): pl.pallas_call(fused_kernel, out_shape=(jax.ShapeDtypeStruct(out_grad.sha...  52.6 us
    pallas_call x1, Pallas kernels, hand_on(): pl.pallas_call(hand_on_kernel, out_shape=tuple((jax.ShapeDtypeStruct(a.sh...  2.78 us

profile of v3, /device:TPU:9, one launch (start us, length us, event | category | flops | bytes accessed | tf_op | source)
XLA Modules:
  0.0 56.7 jit_solution(12467761568001734426)
XLA Ops:
  1.3 52.6 %shard_map.85 = (bf16[64,2048]{1,0:T(8,128)(2,1)}, bf16[128,2048]{1,0:T(8,128)(2,1)}, f32[8,256,256]{2,1,0:T(8,128)}) custom-call(bf16[128,2048]{1,0:T(8,128)(2,1)} %hidden_hbm.1, bf16[1,1,8,256,256]{4,3,2,1,0:T(8,128)(2,1)} %w_hbm.1, s32[1,1,8]{2,1,0:T(1,128)} %rows_hbm.1, s32[1,1,8]{2,1,0:T(1,128)} %cols_hbm.1, s32[1,1]{1,0:T(1,128)S(6)} %copy.9.count_hbm, ...), custom_call_target="tpu_custom_call" | custom-call | tf_op jit(solution)/shard_map/pallas_call | solution.py:429
  53.9 2.8 %shard_map.86 = (bf16[64,2048]{1,0:T(8,128)(2,1)}, bf16[128,2048]{1,0:T(8,128)(2,1)}, f32[8,256,256]{2,1,0:T(8,128)}) custom-call(bf16[64,2048]{1,0:T(8,128)(2,1)} %get-tuple-element.9.p_in, bf16[128,2048]{1,0:T(8,128)(2,1)} %get-tuple-element.10.h_in, f32[8,256,256]{2,1,0:T(8,128)} %get-tuple-element.11.b_in), custom_call_target="tpu_custom_call" | custom-call | tf_op jit(solution)/shard_map/pallas_call | solution.py:410

commit v4 on v3

--- a/solution.py
+++ b/solution.py
@@ -90,7 +90,7 @@
     nc = g_all.shape[0]
     half = nb // 2
     split = half * width
-    pieces = 4
+    pieces = 8
     piece = nc // pieces
     group = hidden_ref.shape[0]
     shard = grad_ref.shape[0]
@@ -464,7 +464,7 @@
             pltpu.SMEM((slots,), jnp.int32),
             pltpu.SMEM((nb,), jnp.int32),
             dma((6,)), dma((6,)), dma((4,)), dma((4,)), dma((4,)), dma((4,)),
-            dma((4,)), dma((4,)), dma((4, 4)), dma((2, 4, 4)), dma((6,)), dma((6,)),
+            dma((4,)), dma((4,)), dma((4, 8)), dma((2, 4, 8)), dma((6,)), dma((6,)),
         ],
         compiler_params=pltpu.CompilerParams(
             collective_id=0, has_side_effects=True, vmem_limit_bytes=56 * 1024 * 1024

time: 56.9 us -> 57.3 us (level)
  no operation moved by 1% of the time
where the time goes in v4:
time: 57.3 us; the launch traced here: 57.1 us
  Pallas kernels  55.8 us (97%)
  between operations  1.29 us (2%)
    pallas_call x1, Pallas kernels, fused_on_device(): pl.pallas_call(fused_kernel, out_shape=(jax.ShapeDtypeStruct(out_grad.sha...  53 us
    pallas_call x1, Pallas kernels, hand_on(): pl.pallas_call(hand_on_kernel, out_shape=tuple((jax.ShapeDtypeStruct(a.sh...  2.78 us

profile of v4, /device:TPU:9, one launch (start us, length us, event | category | flops | bytes accessed | tf_op | source)
XLA Modules:
  0.0 57.1 jit_solution(16258112935955970164)
XLA Ops:
  1.3 53.0 %shard_map.85 = (bf16[64,2048]{1,0:T(8,128)(2,1)}, bf16[128,2048]{1,0:T(8,128)(2,1)}, f32[8,256,256]{2,1,0:T(8,128)}) custom-call(bf16[128,2048]{1,0:T(8,128)(2,1)} %hidden_hbm.1, bf16[1,1,8,256,256]{4,3,2,1,0:T(8,128)(2,1)} %w_hbm.1, s32[1,1,8]{2,1,0:T(1,128)} %rows_hbm.1, s32[1,1,8]{2,1,0:T(1,128)} %cols_hbm.1, s32[1,1]{1,0:T(1,128)S(6)} %copy.9.count_hbm, ...), custom_call_target="tpu_custom_call" | custom-call | tf_op jit(solution)/shard_map/pallas_call | solution.py:429
  54.3 2.8 %shard_map.86 = (bf16[64,2048]{1,0:T(8,128)(2,1)}, bf16[128,2048]{1,0:T(8,128)(2,1)}, f32[8,256,256]{2,1,0:T(8,128)}) custom-call(bf16[64,2048]{1,0:T(8,128)(2,1)} %get-tuple-element.9.p_in, bf16[128,2048]{1,0:T(8,128)(2,1)} %get-tuple-element.10.h_in, f32[8,256,256]{2,1,0:T(8,128)} %get-tuple-element.11.b_in), custom_call_target="tpu_custom_call" | custom-call | tf_op jit(solution)/shard_map/pallas_call | solution.py:410
